TPU v7x, 512 devices: a whole 4x8x8 slice. The times are simulated.
512 devices in a mesh: chan: 128 (over y, z, core), tm: 4 (over x).
Axes of the slice: x: 4, y: 8, z: 8, core: 2. Of those that a mesh axis runs over, the one named last changes fastest.
Arguments:
- samples: float32 [512, 32, 2048], P('chan', 'tm'), may hold values from -6 to 6
- block_owner: int32 [128], replicated, may hold values from 0 to 127, as said below
Outputs:
- correlations: float32 [128, 4, 4, 4, 512], P('chan', None, None, None, 'tm')
Inputs may be any that keep to these rules, and one draw needn't show every extreme that they name: block_owner is a permutation that, for each aligned pair of blocks 2i and 2i + 1, either keeps both or swaps them; at least one pair is swapped.
All inputs are finite; a program needn't handle non-finite values.
Results may differ from a plain program's by a relative error of at most 0.0054.
Values may be sent and summed in bfloat16 or wider, within the bound.
A program may use at most 128 MiB of HBM per device.

v0:
```python
import functools
import math

import jax
import jax.numpy as jnp
import ml_dtypes
import numpy as np
from jax import lax
from jax.experimental import pallas as pl
from jax.experimental.pallas import tpu as pltpu
from jax.sharding import PartitionSpec as P

MESH = pl.DeviceIdType.MESH
NSEG = 2048
LAGS = 512
SMOOTH = 32
BAND = 4
NF = 1024
EPSILON = 1e-06
CH = 4
SEG = 8
ROWS = CH * SEG
LANES = 128
TILE = 16
RADIX = 8
POINTS = NSEG // RADIX
BLOCK = ROWS * TILE
PAIR = CH * CH
N_TM = 4


def tables(segments):
    t2 = np.arange(POINTS)
    radix = np.arange(RADIX)
    angle = 2.0 * math.pi * (radix[:, None] * t2[None, :] % NSEG) / NSEG
    twiddle = np.concatenate([np.cos(angle), np.sin(angle)], 0).astype(np.float32)
    angle = 2.0 * math.pi * (t2[:, None] * np.arange(LANES)[None, :] % POINTS) / POINTS
    cos, sin = np.cos(angle), np.sin(angle)
    dft = np.concatenate(
        [np.concatenate([cos, -sin], 1), np.concatenate([sin, cos], 1)], 0
    ).astype(np.float32)
    bins = radix[:, None] + RADIX * np.arange(LANES)[None, :]
    count = np.minimum(bins, SMOOTH) + np.minimum(NF - 1 - bins, SMOOTH) + 1
    share = (1.0 / count).astype(np.float32)
    lag = np.arange(LAGS) - LAGS // 2
    phase = (bins.reshape(-1)[:, None] * lag[None, :]) % NSEG
    angle = phase.astype(np.float32) * np.float32(2.0 * math.pi / NSEG)
    factor = np.float32(1.0 / math.sqrt(NF))
    lags = np.concatenate([np.cos(angle) * factor, -np.sin(angle) * factor], 0)
    lags = lags.astype(ml_dtypes.bfloat16).astype(np.float32) / np.float32(segments)
    return twiddle, dft, share, lags.astype(ml_dtypes.bfloat16)


def shifted(x, by):
    lane = lax.broadcasted_iota(jnp.int32, x.shape, 1)
    if by > 0:
        return jnp.where(lane >= by, pltpu.roll(x, by, 1), 0.0)
    return jnp.where(lane < LANES + by, pltpu.roll(x, LANES + by, 1), 0.0)


def radix_stage(x, twiddle):
    c = math.sqrt(0.5)
    a0, b0 = x[0] + x[4], x[0] - x[4]
    a1, b1 = x[1] + x[5], x[1] - x[5]
    a2, b2 = x[2] + x[6], x[2] - x[6]
    a3, b3 = x[3] + x[7], x[3] - x[7]
    even, odd = a0 + a2, a1 + a3
    low, high = c * (b1 - b3), c * (b1 + b3)
    y = [
        (even + odd, None),
        (b0 + low, -(b2 + high)),
        (a0 - a2, a3 - a1),
        (b0 - low, b2 - high),
        (even - odd, None),
    ]
    y += [(y[3][0], -y[3][1]), (y[2][0], -y[2][1]), (y[1][0], -y[1][1])]
    out = []
    for k1, (re, im) in enumerate(y):
        cos, sin = twiddle[k1 : k1 + 1, :], twiddle[RADIX + k1 : RADIX + k1 + 1, :]
        if k1 == 0:
            out.append((re, jnp.zeros_like(re)))
        elif im is None:
            out.append((re * cos, -(re * sin)))
        else:
            out.append((re * cos + im * sin, im * cos - re * sin))
    return out


def whiten(samples, twiddle, dft, share, z, y, rows):
    x = [samples[:, :, t * POINTS : (t + 1) * POINTS].reshape(ROWS, POINTS) for t in range(RADIX)]
    total = ((x[0] + x[1]) + (x[2] + x[3])) + ((x[4] + x[5]) + (x[6] + x[7]))
    mean = jnp.sum(total, axis=1, keepdims=True) * (1.0 / NSEG)
    x = [part - mean for part in x]
    for k1, (re, im) in enumerate(radix_stage(x, twiddle)):
        z[k1 * ROWS : (k1 + 1) * ROWS, :POINTS] = re
        z[k1 * ROWS : (k1 + 1) * ROWS, POINTS:] = im
    y[...] = jnp.dot(
        z[...], dft[...], precision=lax.Precision.HIGHEST, preferred_element_type=jnp.float32
    )
    re = [y[m * ROWS : (m + 1) * ROWS, :LANES] for m in range(RADIX)]
    im = [y[m * ROWS : (m + 1) * ROWS, LANES:] for m in range(RADIX)]
    size = [jnp.sqrt(r * r + i * i) for r, i in zip(re, im)]
    before, after = [size[0]], [size[-1]]
    for m in range(1, RADIX):
        before.append(before[-1] + size[m])
        after.append(after[-1] + size[RADIX - 1 - m])
    after = after[::-1]
    whole = before[-1]
    middle = whole
    for by in (1, 2, 3):
        middle = middle + (shifted(whole, by) + shifted(whole, -by))
    for m in range(RADIX):
        window = middle + (shifted(before[m], -4) + shifted(after[m], 4))
        scale = 1.0 / (window * share[m : m + 1, :] + EPSILON)
        rows[pl.ds(m, ROWS, stride=TILE), :] = re[m] * scale
        rows[pl.ds(RADIX + m, ROWS, stride=TILE), :] = im[m] * scale


def pair_cross(white, left, right, cross, place):
    def body(s, total):
        def halves(slot, channel):
            start = pl.multiple_of(slot * BLOCK + (channel * SEG + s) * TILE, TILE)
            tile = white[pl.ds(start, TILE), :].astype(jnp.float32)
            return tile[:RADIX, :], tile[RADIX:, :]

        lefts = [halves(left, i) for i in range(CH)]
        rights = [halves(right, j) for j in range(CH)]
        out = []
        for i in range(CH):
            for j in range(CH):
                (lr, li), (rr, ri) = lefts[i], rights[j]
                re, im = total[2 * (i * CH + j)], total[2 * (i * CH + j) + 1]
                out.append(re + (lr * rr + li * ri))
                out.append(im + (li * rr - lr * ri))
        return tuple(out)

    zero = jnp.zeros((RADIX, LANES), jnp.float32)
    total = lax.fori_loop(0, SEG, body, (zero,) * (2 * PAIR))
    for p in range(PAIR):
        start = (place * PAIR + p) * TILE
        cross[start : start + RADIX, :] = total[2 * p]
        cross[start + RADIX : start + TILE, :] = total[2 * p + 1]


def kernel(
    chips, samples_ref, owner_ref, twiddle_ref, dft_ref, share_ref, lags_ref, out_ref,
    samples, twiddle, dft, share, lags, z, y, rows, white, cross, result,
    from_a, from_x, from_b, from_y,
    load_sem, send_sem, recv_sem, sum_send, sum_recv,
):
    position, t = lax.axis_index("chan"), lax.axis_index("tm")
    q, e = position // 2, lax.rem(position, 2)
    after, before = lax.rem(q + 1, chips), lax.rem(q + chips - 1, chips)

    def device(chip, core, row):
        return (chip * 2 + core, row)

    def other(step):
        return lax.rem(t + step, N_TM)

    barrier = pltpu.get_barrier_semaphore()

    def greet(target):
        pl.semaphore_signal(barrier, inc=1, device_id=target, device_id_type=MESH)

    greet(device(q, 1 - e, t))
    greet(device(before, e, t))
    for core in (0, 1):
        greet(device(after, core, t))
        for step in range(1, N_TM):
            greet(device(q, core, other(step)))
            greet(device(after, core, other(step)))

    loads = [
        pltpu.make_async_copy(src, dst, load_sem.at[n])
        for n, (src, dst) in enumerate(
            [(samples_ref, samples), (twiddle_ref, twiddle), (dft_ref, dft), (share_ref, share),
             (lags_ref, lags)]
        )
    ]
    for load in loads:
        load.start()
    for load in loads[:4]:
        load.wait()

    whiten(samples, twiddle, dft, share, z, y, rows)
    own = pl.ds(pl.multiple_of(e * BLOCK, BLOCK), BLOCK)
    white[own, :] = rows[...].astype(jnp.bfloat16)

    pl.semaphore_wait(barrier, 2 + 2 + 4 * (N_TM - 1))

    def send(slot, n, target):
        place = pl.ds(pl.multiple_of(slot * BLOCK, BLOCK), BLOCK)
        return pltpu.make_async_remote_copy(
            src_ref=white.at[own, :], dst_ref=white.at[place, :], send_sem=send_sem.at[n],
            recv_sem=recv_sem.at[n], device_id=target, device_id_type=MESH,
        )

    copies = [
        send(4, 0, device(before, e, t)),
        send(2 + e, 1, device(after, e, t)),
        send(e, 2, device(q, 1 - e, t)),
    ]
    for copy in copies:
        copy.start()
    passed = pl.ds(3 * BLOCK, BLOCK)
    pass_on = pltpu.make_async_remote_copy(
        src_ref=white.at[passed, :], dst_ref=white.at[passed, :], send_sem=send_sem.at[3],
        recv_sem=recv_sem.at[3], device_id=device(q, 1 - e, t), device_id_type=MESH,
    )
    for copy in copies:
        copy.wait_recv()

    @pl.when(e == 1)
    def _():
        pass_on.start()

    pair_cross(white, 0, 4, cross, 0)
    pair_cross(white, 1, 4, cross, 1)
    pair_cross(white, 2 * (1 - e), 4 - 3 * e, cross, 2)

    @pl.when(e == 0)
    def _():
        pass_on.wait_recv()

    pair_cross(white, 3, 4, cross, 3)

    loads[4].wait()
    parts = [
        cross[pl.ds(n, BAND * PAIR, stride=TILE), :].astype(jnp.bfloat16) for n in range(TILE)
    ]
    corr = jnp.dot(
        jnp.concatenate(parts, axis=1), lags[...], preferred_element_type=jnp.float32
    )

    swap = owner_ref[2 * q] != 2 * q
    swap_before = owner_ref[2 * before] != 2 * before
    r = [corr[n * PAIR : (n + 1) * PAIR, :] for n in range(BAND)]
    first = jnp.where(swap, r[1], r[0])
    second = jnp.where(swap, r[0], r[1])

    def put(place, value):
        for row in range(N_TM):
            result[row, place * PAIR : (place + 1) * PAIR, :] = value[
                :, row * LANES : (row + 1) * LANES
            ]

    put(0, first)

    @pl.when(e == 0)
    def _():
        put(1, second)
        put(2, jnp.where(swap_before, r[3], r[2]))
        put(3, jnp.where(swap_before, r[2], r[3]))

    @pl.when(e == 1)
    def _():
        put(1, r[2])
        put(2, second)
        put(3, r[3])

    def handed(core, step):
        row = other(step)
        if core == 0:
            plan = [(0, 1, from_a, 0), (1, 1, from_a, 0), (2, 1, from_b, 2), (3, 1, from_b, 2)]
        else:
            plan = [(0, 2, from_x, 1), (1, 2, from_x, 1), (3, 1, from_y, 3), (3, 1, from_y, 3)]
        sends = []
        for n, (place, size, buffer, kind) in enumerate(plan):
            if n < 2 and step == 0 and n == core:
                continue
            sends.append(
                pltpu.make_async_remote_copy(
                    src_ref=result.at[row, pl.ds(place * PAIR, size * PAIR), :],
                    dst_ref=buffer.at[t],
                    send_sem=sum_send.at[step, n],
                    recv_sem=sum_recv.at[kind, t],
                    device_id=device(q if n < 2 else before, n % 2, row),
                    device_id_type=MESH,
                )
            )
        return sends

    for core in (0, 1):

        @pl.when(e == core)
        def _():
            sends = []
            for step in (2, 1, 3, 0):
                sends += handed(core, step)
            for copy in sends:
                copy.start()
            if core == 0:
                from_a[t] = result[t, :PAIR, :]
            else:
                from_x[t] = result[t, PAIR : 3 * PAIR, :]
            for copy in sends:
                copy.wait_send()

    def arrived(size, buffer, n, row):
        return pltpu.make_async_remote_copy(
            src_ref=result.at[0, pl.ds(0, size), :], dst_ref=buffer.at[row],
            send_sem=sum_send.at[0, n], recv_sem=sum_recv.at[n, row],
            device_id=device(q, 1 - e, t), device_id_type=MESH,
        )

    for step in range(N_TM):
        row = other(step)
        if step > 0:
            arrived(PAIR, from_a, 0, row).wait_recv()
            arrived(2 * PAIR, from_x, 1, row).wait_recv()
        arrived(PAIR, from_b, 2, row).wait_recv()
        arrived(PAIR, from_y, 3, row).wait_recv()

    @pl.when(e == 1)
    def _():
        arrived(PAIR, from_a, 0, t).wait_recv()

    @pl.when(e == 0)
    def _():
        arrived(2 * PAIR, from_x, 1, t).wait_recv()

    def summed(buffer):
        return (buffer[0] + buffer[1]) + (buffer[2] + buffer[3])

    a, x, b, last = summed(from_a), summed(from_x), summed(from_b), summed(from_y)
    flip = e == 1
    right = jnp.where(flip, x[PAIR:], x[:PAIR])
    inner = jnp.where(flip, x[:PAIR], x[PAIR:])
    odd = jnp.logical_xor(swap, e == 1)
    block = 2 * q + odd.astype(jnp.int32)
    low = [inner, a, right, b]
    high = [a, right, b, last]
    for n in range(BAND):
        value = jnp.where(odd, high[n], low[n])
        out_ref[n * PAIR : (n + 1) * PAIR, :] = jnp.where(
            block + n + 1 < 2 * chips, value, jnp.zeros_like(value)
        )

    for copy in copies:
        copy.wait_send()

    @pl.when(e == 1)
    def _():
        pass_on.wait_send()


def shards(chips, samples, block_owner):
    segments = samples.shape[1] * N_TM
    twiddle, dft, share, lags = tables(segments)
    anywhere = pl.BlockSpec(memory_space=pl.ANY)
    out = pl.pallas_call(
        functools.partial(kernel, chips),
        out_shape=jax.ShapeDtypeStruct((BAND * PAIR, LANES), jnp.float32),
        in_specs=[anywhere, pl.BlockSpec(memory_space=pltpu.SMEM)] + [anywhere] * 4,
        out_specs=pl.BlockSpec(memory_space=pltpu.VMEM),
        scratch_shapes=[
            pltpu.VMEM((CH, SEG, NSEG), jnp.float32),
            pltpu.VMEM(twiddle.shape, jnp.float32),
            pltpu.VMEM(dft.shape, jnp.float32),
            pltpu.VMEM(share.shape, jnp.float32),
            pltpu.VMEM(lags.shape, jnp.bfloat16),
            pltpu.VMEM((RADIX * ROWS, 2 * POINTS), jnp.float32),
            pltpu.VMEM((RADIX * ROWS, 2 * LANES), jnp.float32),
            pltpu.VMEM((BLOCK, LANES), jnp.float32),
            pltpu.VMEM((5 * BLOCK, LANES), jnp.bfloat16),
            pltpu.VMEM((BAND * PAIR * TILE, LANES), jnp.float32),
            pltpu.VMEM((N_TM, BAND * PAIR, LANES), jnp.float32),
            pltpu.VMEM((N_TM, PAIR, LANES), jnp.float32),
            pltpu.VMEM((N_TM, 2 * PAIR, LANES), jnp.float32),
            pltpu.VMEM((N_TM, PAIR, LANES), jnp.float32),
            pltpu.VMEM((N_TM, PAIR, LANES), jnp.float32),
            pltpu.SemaphoreType.DMA((5,)),
            pltpu.SemaphoreType.DMA((4,)),
            pltpu.SemaphoreType.DMA((4,)),
            pltpu.SemaphoreType.DMA((N_TM, 4)),
            pltpu.SemaphoreType.DMA((4, N_TM)),
        ],
        compiler_params=pltpu.CompilerParams(
            collective_id=0, has_side_effects=True, vmem_limit_bytes=32 * 1024 * 1024
        ),
    )(
        samples, block_owner, jnp.asarray(twiddle), jnp.asarray(dft), jnp.asarray(share),
        jnp.asarray(lags),
    )
    return out.reshape(1, BAND, CH, CH, LANES)


def solution(mesh):
    in_specs = (P("chan", "tm", None), P())
    out_specs = P("chan", None, None, None, "tm")
    chips = mesh.shape["chan"] // 2
    return jax.shard_map(
        functools.partial(shards, chips), mesh=mesh, in_specs=in_specs, out_specs=out_specs,
        check_vma=False,
    )
```

profile of v0, /device:TPU:1, one launch (start us, length us, event | category | flops | bytes accessed | tf_op | source)
XLA Modules:
  0.0 33.6 jit_solution(2269538305083110938)
XLA Ops:
  0.0 0.0 copy-start
  0.0 1.6 %copy-done = bf16[2048,512]{1,0:T(8,128)(2,1)S(1)} copy-done((bf16[2048,512]{1,0:T(8,128)(2,1)S(1)}, bf16[2048,512]{1,0:T(8,128)(2,1)}, u32[]{:S(2)}) %copy-start) | copy-done | bytes 2097176
  1.6 0.0 copy-start.1
  1.6 1.0 %copy-done.1 = f32[512,256]{1,0:T(8,128)S(1)} copy-done((f32[512,256]{1,0:T(8,128)S(1)}, f32[512,256]{1,0:T(8,128)}, u32[]{:S(2)}) %copy-start.1) | copy-done | bytes 524312
  2.6 0.0 copy-start.2
  2.6 0.9 %copy-done.2 = f32[4,8,2048]{2,1,0:T(8,128)S(1)} copy-done((f32[4,8,2048]{2,1,0:T(8,128)S(1)}, f32[4,8,2048]{2,1,0:T(8,128)}, u32[]{:S(2)}) %copy-start.2) | copy-done | bytes 262168
  3.6 0.0 copy-start.3
  3.6 0.7 %copy-done.3 = f32[16,256]{1,0:T(8,128)S(1)} copy-done((f32[16,256]{1,0:T(8,128)S(1)}, f32[16,256]{1,0:T(8,128)}, u32[]{:S(2)}) %copy-start.3) | copy-done | bytes 16408
  4.3 0.0 copy-start.4
  4.3 0.7 %copy-done.4 = f32[8,128]{1,0:T(8,128)S(1)} copy-done((f32[8,128]{1,0:T(8,128)S(1)}, f32[8,128]{1,0:T(8,128)}, u32[]{:S(2)}) %copy-start.4) | copy-done | bytes 4120
  5.0 0.0 copy-start.5
  5.0 0.7 %copy-done.5 = s32[128]{0:T(128)S(1)} copy-done((s32[128]{0:T(128)S(1)}, s32[128]{0:T(128)}, u32[]{:S(2)}) %copy-start.5) | copy-done | bytes 536
  5.6 27.3 %shard_map.64 = f32[64,128]{1,0:T(8,128)S(1)} custom-call(f32[4,8,2048]{2,1,0:T(8,128)S(1)} %copy-done.2, s32[128]{0:T(128)S(1)} %copy-done.5, f32[16,256]{1,0:T(8,128)S(1)} %copy-done.3, f32[512,256]{1,0:T(8,128)S(1)} %copy-done.1, f32[8,128]{1,0:T(8,128)S(1)} %copy-done.4, bf16[2048,512]{1,0:T(8,128)(2,1)S(1)} %copy-done), custom_call_target="tpu_custom_call" | custom-call | tf_op jit(solution)/shard_map/pallas_call | solution.py:352
  33.0 0.6 %copy.8 = f32[1,4,4,4,128]{4,3,2,1,0:T(4,128)} copy(f32[1,4,4,4,128]{4,3,2,1,0:T(4,128)S(1)} %bitcast.1) | data formatting | bytes 65536
Async XLA Ops:
  0.0 1.6 %copy-start = (bf16[2048,512]{1,0:T(8,128)(2,1)S(1)}, bf16[2048,512]{1,0:T(8,128)(2,1)}, u32[]{:S(2)}) copy-start(bf16[2048,512]{1,0:T(8,128)(2,1)} %constant.11.clone.lags_ref) | copy-start | bytes 6291460
  1.6 1.0 %copy-start.1 = (f32[512,256]{1,0:T(8,128)S(1)}, f32[512,256]{1,0:T(8,128)}, u32[]{:S(2)}) copy-start(f32[512,256]{1,0:T(8,128)} %constant.9.clone.dft_ref) | copy-start | bytes 1572868
  2.6 0.9 %copy-start.2 = (f32[4,8,2048]{2,1,0:T(8,128)S(1)}, f32[4,8,2048]{2,1,0:T(8,128)}, u32[]{:S(2)}) copy-start(f32[4,8,2048]{2,1,0:T(8,128)} %samples_ref.1) | copy-start | bytes 786436
  3.6 0.7 %copy-start.3 = (f32[16,256]{1,0:T(8,128)S(1)}, f32[16,256]{1,0:T(8,128)}, u32[]{:S(2)}) copy-start(f32[16,256]{1,0:T(8,128)} %constant.8.clone.twiddle_ref) | copy-start | bytes 49156
  4.3 0.7 %copy-start.4 = (f32[8,128]{1,0:T(8,128)S(1)}, f32[8,128]{1,0:T(8,128)}, u32[]{:S(2)}) copy-start(f32[8,128]{1,0:T(8,128)} %constant.10.clone.share_ref) | copy-start | bytes 12292
  5.0 0.7 %copy-start.5 = (s32[128]{0:T(128)S(1)}, s32[128]{0:T(128)}, u32[]{:S(2)}) copy-start(s32[128]{0:T(128)} %owner_ref.1) | copy-start | bytes 1540
where the time goes:
time: 33.9 us; the launch traced here: 33.6 us
  Pallas kernels  27.3 us (81%)
  local copies, waits for them, and re-layouts  6.26 us (18%)
    pallas_call x1, Pallas kernels, shards(): pl.pallas_call(functools.partial(kernel, chips), out_shape=jax.ShapeDtype...  27.3 us
    unnamed x13, local copies, waits for them, and re-layouts  6.26 us

commit v1 on v0

--- a/solution.py
+++ b/solution.py
@@ -42,13 +42,14 @@
     bins = radix[:, None] + RADIX * np.arange(LANES)[None, :]
     count = np.minimum(bins, SMOOTH) + np.minimum(NF - 1 - bins, SMOOTH) + 1
     share = (1.0 / count).astype(np.float32)
+    angle = 2.0 * math.pi * (np.arange(LANES)[:, None] * np.arange(POINTS)[None, :] % POINTS) / POINTS
+    cos, sin = np.cos(angle), np.sin(angle)
+    inner = np.concatenate([np.concatenate([cos, sin], 1), np.concatenate([-sin, cos], 1)], 0)
     lag = np.arange(LAGS) - LAGS // 2
-    phase = (bins.reshape(-1)[:, None] * lag[None, :]) % NSEG
-    angle = phase.astype(np.float32) * np.float32(2.0 * math.pi / NSEG)
-    factor = np.float32(1.0 / math.sqrt(NF))
-    lags = np.concatenate([np.cos(angle) * factor, -np.sin(angle) * factor], 0)
-    lags = lags.astype(ml_dtypes.bfloat16).astype(np.float32) / np.float32(segments)
-    return twiddle, dft, share, lags.astype(ml_dtypes.bfloat16)
+    angle = 2.0 * math.pi * (radix[:, None] * lag[None, :] % NSEG) / NSEG
+    factor = 1.0 / (math.sqrt(NF) * segments)
+    outer = np.concatenate([np.cos(angle), np.sin(angle)], 0) * factor
+    return twiddle, dft, share, inner.astype(ml_dtypes.bfloat16), outer.astype(np.float32)
 
 
 def shifted(x, by):
@@ -116,7 +117,7 @@
         rows[pl.ds(RADIX + m, ROWS, stride=TILE), :] = im[m] * scale
 
 
-def pair_cross(white, left, right, cross, place):
+def pair_cross(white, left, right, cross):
     def body(s, total):
         def halves(slot, channel):
             start = pl.multiple_of(slot * BLOCK + (channel * SEG + s) * TILE, TILE)
@@ -137,16 +138,39 @@
     zero = jnp.zeros((RADIX, LANES), jnp.float32)
     total = lax.fori_loop(0, SEG, body, (zero,) * (2 * PAIR))
     for p in range(PAIR):
-        start = (place * PAIR + p) * TILE
-        cross[start : start + RADIX, :] = total[2 * p]
-        cross[start + RADIX : start + TILE, :] = total[2 * p + 1]
+        cross[p * RADIX : (p + 1) * RADIX, :] = total[2 * p]
+        cross[(PAIR + p) * RADIX : (PAIR + p + 1) * RADIX, :] = total[2 * p + 1]
+
+
+def pair_lags(white, left, right, cross, inner, outer):
+    pair_cross(white, left, right, cross)
+    re = [cross[pl.ds(m, PAIR, stride=RADIX), :] for m in range(RADIX)]
+    im = [cross[pl.ds(PAIR * RADIX + m, PAIR, stride=RADIX), :] for m in range(RADIX)]
+    parts = [jnp.concatenate(re, axis=0), jnp.concatenate(im, axis=0)]
+    spread = jnp.dot(
+        jnp.concatenate(parts, axis=1).astype(jnp.bfloat16),
+        inner[...],
+        preferred_element_type=jnp.float32,
+    )
+    out = []
+    for row in range(N_TM):
+        total = None
+        for m in range(RADIX):
+            lanes = slice(row * LANES, (row + 1) * LANES)
+            at = row % 2 * LANES
+            re = spread[m * PAIR : (m + 1) * PAIR, at : at + LANES]
+            im = spread[m * PAIR : (m + 1) * PAIR, POINTS + at : POINTS + at + LANES]
+            term = re * outer[m : m + 1, lanes] - im * outer[RADIX + m : RADIX + m + 1, lanes]
+            total = term if total is None else total + term
+        out.append(total)
+    return out
 
 
 def kernel(
-    chips, samples_ref, owner_ref, twiddle_ref, dft_ref, share_ref, lags_ref, out_ref,
-    samples, twiddle, dft, share, lags, z, y, rows, white, cross, result,
+    chips, samples_ref, owner_ref, twiddle_ref, dft_ref, share_ref, inner_ref, outer_ref, out_ref,
+    samples, twiddle, dft, share, inner, outer, owner, z, y, rows, white, cross, result,
     from_a, from_x, from_b, from_y,
-    load_sem, send_sem, recv_sem, sum_send, sum_recv,
+    load_sem, send_sem, recv_sem, sum_send, sum_recv, ready,
 ):
     position, t = lax.axis_index("chan"), lax.axis_index("tm")
     q, e = position // 2, lax.rem(position, 2)
@@ -163,31 +187,43 @@
     def greet(target):
         pl.semaphore_signal(barrier, inc=1, device_id=target, device_id_type=MESH)
 
+    has_before, has_after = q > 0, q < chips - 1
+
+    @pl.when(has_before)
+    def _():
+        greet(device(before, 1, t))
+
+    @pl.when(jnp.logical_and(has_before, e == 0))
+    def _():
+        greet(device(before, 0, t))
+
     greet(device(q, 1 - e, t))
-    greet(device(before, e, t))
-    for core in (0, 1):
-        greet(device(after, core, t))
-        for step in range(1, N_TM):
+    for step in range(1, N_TM):
+        for core in (0, 1):
             greet(device(q, core, other(step)))
-            greet(device(after, core, other(step)))
 
     loads = [
         pltpu.make_async_copy(src, dst, load_sem.at[n])
         for n, (src, dst) in enumerate(
             [(samples_ref, samples), (twiddle_ref, twiddle), (dft_ref, dft), (share_ref, share),
-             (lags_ref, lags)]
+             (inner_ref, inner), (outer_ref, outer), (owner_ref, owner)]
         )
     ]
     for load in loads:
         load.start()
+    last = q // (chips - 1)
+    pl.semaphore_wait(barrier, 1 + 2 * (N_TM - 1) + (1 - last) * (1 + e))
+
+    @pl.when(has_after)
+    def _():
+        pl.semaphore_signal(ready, inc=1, device_id=device(after, e, t), device_id_type=MESH)
+
     for load in loads[:4]:
         load.wait()
 
     whiten(samples, twiddle, dft, share, z, y, rows)
     own = pl.ds(pl.multiple_of(e * BLOCK, BLOCK), BLOCK)
     white[own, :] = rows[...].astype(jnp.bfloat16)
-
-    pl.semaphore_wait(barrier, 2 + 2 + 4 * (N_TM - 1))
 
     def send(slot, n, target):
         place = pl.ds(pl.multiple_of(slot * BLOCK, BLOCK), BLOCK)
@@ -196,106 +232,121 @@
             recv_sem=recv_sem.at[n], device_id=target, device_id_type=MESH,
         )
 
-    copies = [
-        send(4, 0, device(before, e, t)),
-        send(2 + e, 1, device(after, e, t)),
-        send(e, 2, device(q, 1 - e, t)),
-    ]
-    for copy in copies:
-        copy.start()
-    passed = pl.ds(3 * BLOCK, BLOCK)
-    pass_on = pltpu.make_async_remote_copy(
-        src_ref=white.at[passed, :], dst_ref=white.at[passed, :], send_sem=send_sem.at[3],
-        recv_sem=recv_sem.at[3], device_id=device(q, 1 - e, t), device_id_type=MESH,
-    )
-    for copy in copies:
-        copy.wait_recv()
-
-    @pl.when(e == 1)
-    def _():
-        pass_on.start()
-
-    pair_cross(white, 0, 4, cross, 0)
-    pair_cross(white, 1, 4, cross, 1)
-    pair_cross(white, 2 * (1 - e), 4 - 3 * e, cross, 2)
-
-    @pl.when(e == 0)
-    def _():
-        pass_on.wait_recv()
-
-    pair_cross(white, 3, 4, cross, 3)
-
-    loads[4].wait()
-    parts = [
-        cross[pl.ds(n, BAND * PAIR, stride=TILE), :].astype(jnp.bfloat16) for n in range(TILE)
-    ]
-    corr = jnp.dot(
-        jnp.concatenate(parts, axis=1), lags[...], preferred_element_type=jnp.float32
-    )
-
-    swap = owner_ref[2 * q] != 2 * q
-    swap_before = owner_ref[2 * before] != 2 * before
-    r = [corr[n * PAIR : (n + 1) * PAIR, :] for n in range(BAND)]
-    first = jnp.where(swap, r[1], r[0])
-    second = jnp.where(swap, r[0], r[1])
+    to_after = send(2 + e, 1, device(after, e, t))
+    to_after_other = send(3, 3, device(after, 0, t))
+    to_other = send(e, 2, device(q, 1 - e, t))
+    to_before = send(4, 0, device(before, e, t))
 
     def put(place, value):
         for row in range(N_TM):
-            result[row, place * PAIR : (place + 1) * PAIR, :] = value[
-                :, row * LANES : (row + 1) * LANES
-            ]
-
-    put(0, first)
-
-    @pl.when(e == 0)
-    def _():
-        put(1, second)
-        put(2, jnp.where(swap_before, r[3], r[2]))
-        put(3, jnp.where(swap_before, r[2], r[3]))
-
-    @pl.when(e == 1)
-    def _():
-        put(1, r[2])
-        put(2, second)
-        put(3, r[3])
-
-    def handed(core, step):
+            result[row, place * PAIR : (place + 1) * PAIR, :] = value[row]
+
+    def chosen(by, yes, no):
+        return [jnp.where(by, a, b) for a, b in zip(yes, no)]
+
+    def lagged(left, right):
+        return pair_lags(white, left, right, cross, inner, outer)
+
+    def hand(core, step, n):
         row = other(step)
         if core == 0:
-            plan = [(0, 1, from_a, 0), (1, 1, from_a, 0), (2, 1, from_b, 2), (3, 1, from_b, 2)]
+            place, size, buffer, kind = n, 1, (from_a, from_b)[n // 2], n // 2 * 2
         else:
-            plan = [(0, 2, from_x, 1), (1, 2, from_x, 1), (3, 1, from_y, 3), (3, 1, from_y, 3)]
-        sends = []
-        for n, (place, size, buffer, kind) in enumerate(plan):
-            if n < 2 and step == 0 and n == core:
-                continue
-            sends.append(
-                pltpu.make_async_remote_copy(
-                    src_ref=result.at[row, pl.ds(place * PAIR, size * PAIR), :],
-                    dst_ref=buffer.at[t],
-                    send_sem=sum_send.at[step, n],
-                    recv_sem=sum_recv.at[kind, t],
-                    device_id=device(q if n < 2 else before, n % 2, row),
-                    device_id_type=MESH,
-                )
-            )
-        return sends
-
-    for core in (0, 1):
-
-        @pl.when(e == core)
-        def _():
-            sends = []
-            for step in (2, 1, 3, 0):
-                sends += handed(core, step)
-            for copy in sends:
-                copy.start()
-            if core == 0:
-                from_a[t] = result[t, :PAIR, :]
-            else:
-                from_x[t] = result[t, PAIR : 3 * PAIR, :]
-            for copy in sends:
+            place, size = (0, 1, 3, 3)[n], 2 - n // 2
+            buffer, kind = (from_x, from_y)[n // 2], 1 + n // 2 * 2
+        return pltpu.make_async_remote_copy(
+            src_ref=result.at[row, pl.ds(place * PAIR, size * PAIR), :],
+            dst_ref=buffer.at[t],
+            send_sem=sum_send.at[step, n],
+            recv_sem=sum_recv.at[kind, t],
+            device_id=device(q if n < 2 else before, n % 2, row),
+            device_id_type=MESH,
+        )
+
+    def hands(core, targets):
+        return [
+            hand(core, step, n)
+            for step in (2, 1, 3, 0)
+            for n in targets
+            if step > 0 or n != core
+        ]
+
+    def start(copies):
+        for copy in copies:
+            copy.start()
+        return copies
+
+    loads[4].wait()
+    loads[5].wait()
+    loads[6].wait()
+    swap = owner[2 * q] != 2 * q
+    swap_before = owner[2 * before] != 2 * before
+
+    to_other.start()
+
+    @pl.when(has_after)
+    def _():
+        @pl.when(e == 1)
+        def _():
+            to_after_other.start()
+
+        to_after.start()
+
+    @pl.when(has_before)
+    def _():
+        pl.semaphore_wait(ready, 1)
+        to_before.start()
+
+    to_other.wait_recv()
+
+    @pl.when(e == 0)
+    def _():
+        @pl.when(has_after)
+        def _():
+            to_before.wait_recv()
+
+        one, two = lagged(0, 4), lagged(1, 4)
+        put(0, chosen(swap, two, one))
+        put(1, chosen(swap, one, two))
+        near = start(hands(0, (0, 1)))
+        from_a[t] = result[t, :PAIR, :]
+
+        @pl.when(has_before)
+        def _():
+            to_after.wait_recv()
+            to_after_other.wait_recv()
+            one, two = lagged(2, 4), lagged(3, 4)
+            put(2, chosen(swap_before, two, one))
+            put(3, chosen(swap_before, one, two))
+            for copy in start(hands(0, (2, 3))):
                 copy.wait_send()
+
+        for copy in near:
+            copy.wait_send()
+
+    @pl.when(e == 1)
+    def _():
+        put(1, lagged(0, 1))
+
+        @pl.when(has_after)
+        def _():
+            to_before.wait_recv()
+
+        one, two = lagged(0, 4), lagged(1, 4)
+        put(0, chosen(swap, two, one))
+        put(2, chosen(swap, one, two))
+        near = start(hands(1, (0, 1)))
+        from_x[t] = result[t, PAIR : 3 * PAIR, :]
+
+        @pl.when(has_before)
+        def _():
+            to_after.wait_recv()
+            put(3, lagged(3, 4))
+            for copy in start(hands(1, (2, 3))):
+                copy.wait_send()
+
+        for copy in near:
+            copy.wait_send()
 
     def arrived(size, buffer, n, row):
         return pltpu.make_async_remote_copy(
@@ -309,8 +360,12 @@
         if step > 0:
             arrived(PAIR, from_a, 0, row).wait_recv()
             arrived(2 * PAIR, from_x, 1, row).wait_recv()
-        arrived(PAIR, from_b, 2, row).wait_recv()
-        arrived(PAIR, from_y, 3, row).wait_recv()
+
+    @pl.when(has_after)
+    def _():
+        for row in range(N_TM):
+            arrived(PAIR, from_b, 2, row).wait_recv()
+            arrived(PAIR, from_y, 3, row).wait_recv()
 
     @pl.when(e == 1)
     def _():
@@ -337,51 +392,59 @@
             block + n + 1 < 2 * chips, value, jnp.zeros_like(value)
         )
 
-    for copy in copies:
-        copy.wait_send()
-
-    @pl.when(e == 1)
-    def _():
-        pass_on.wait_send()
+    to_other.wait_send()
+
+    @pl.when(has_before)
+    def _():
+        to_before.wait_send()
+
+    @pl.when(has_after)
+    def _():
+        to_after.wait_send()
+
+        @pl.when(e == 1)
+        def _():
+            to_after_other.wait_send()
 
 
 def shards(chips, samples, block_owner):
     segments = samples.shape[1] * N_TM
-    twiddle, dft, share, lags = tables(segments)
-    anywhere = pl.BlockSpec(memory_space=pl.ANY)
+    twiddle, dft, share, inner, outer = tables(segments)
+    stay = pl.BlockSpec(memory_space=pltpu.HBM)
     out = pl.pallas_call(
         functools.partial(kernel, chips),
         out_shape=jax.ShapeDtypeStruct((BAND * PAIR, LANES), jnp.float32),
-        in_specs=[anywhere, pl.BlockSpec(memory_space=pltpu.SMEM)] + [anywhere] * 4,
+        in_specs=[stay] * 7,
         out_specs=pl.BlockSpec(memory_space=pltpu.VMEM),
         scratch_shapes=[
             pltpu.VMEM((CH, SEG, NSEG), jnp.float32),
             pltpu.VMEM(twiddle.shape, jnp.float32),
             pltpu.VMEM(dft.shape, jnp.float32),
             pltpu.VMEM(share.shape, jnp.float32),
-            pltpu.VMEM(lags.shape, jnp.bfloat16),
+            pltpu.VMEM(inner.shape, jnp.bfloat16),
+            pltpu.VMEM(outer.shape, jnp.float32),
+            pltpu.SMEM(block_owner.shape, jnp.int32),
             pltpu.VMEM((RADIX * ROWS, 2 * POINTS), jnp.float32),
             pltpu.VMEM((RADIX * ROWS, 2 * LANES), jnp.float32),
             pltpu.VMEM((BLOCK, LANES), jnp.float32),
             pltpu.VMEM((5 * BLOCK, LANES), jnp.bfloat16),
-            pltpu.VMEM((BAND * PAIR * TILE, LANES), jnp.float32),
+            pltpu.VMEM((2 * PAIR * RADIX, LANES), jnp.float32),
             pltpu.VMEM((N_TM, BAND * PAIR, LANES), jnp.float32),
             pltpu.VMEM((N_TM, PAIR, LANES), jnp.float32),
             pltpu.VMEM((N_TM, 2 * PAIR, LANES), jnp.float32),
             pltpu.VMEM((N_TM, PAIR, LANES), jnp.float32),
             pltpu.VMEM((N_TM, PAIR, LANES), jnp.float32),
-            pltpu.SemaphoreType.DMA((5,)),
+            pltpu.SemaphoreType.DMA((7,)),
             pltpu.SemaphoreType.DMA((4,)),
             pltpu.SemaphoreType.DMA((4,)),
             pltpu.SemaphoreType.DMA((N_TM, 4)),
             pltpu.SemaphoreType.DMA((4, N_TM)),
+            pltpu.SemaphoreType.REGULAR,
         ],
-        compiler_params=pltpu.CompilerParams(
-            collective_id=0, has_side_effects=True, vmem_limit_bytes=32 * 1024 * 1024
-        ),
+        compiler_params=pltpu.CompilerParams(collective_id=0, has_side_effects=True),
     )(
         samples, block_owner, jnp.asarray(twiddle), jnp.asarray(dft), jnp.asarray(share),
-        jnp.asarray(lags),
+        jnp.asarray(inner), jnp.asarray(outer),
     )
     return out.reshape(1, BAND, CH, CH, LANES)
 

time: 33.9 us -> 24.5 us (0.72)
  the two profiles are of different devices: /device:TPU:1 before, /device:TPU:48 now
where the time goes in v1:
time: 24.5 us; the launch traced here: 24.4 us
  Pallas kernels  23 us (94%)
  local copies, waits for them, and re-layouts  1.38 us (6%)
    pallas_call x1, Pallas kernels, shards(): pl.pallas_call(functools.partial(kernel, chips), out_shape=jax.ShapeDtype...  23 us
    unnamed x1, local copies, waits for them, and re-layouts  1.38 us

profile of v1, /device:TPU:48, one launch (start us, length us, event | category | flops | bytes accessed | tf_op | source)
XLA Modules:
  0.0 24.4 jit_solution(8600281967892776739)
XLA Ops:
  0.0 23.0 %shard_map.73 = f32[64,128]{1,0:T(8,128)} custom-call(f32[4,8,2048]{2,1,0:T(8,128)} %samples_ref.1, s32[128]{0:T(128)} %owner_ref.1, f32[16,256]{1,0:T(8,128)} %constant.10.clone.twiddle_ref, f32[512,256]{1,0:T(8,128)} %constant.11.clone.dft_ref, f32[8,128]{1,0:T(8,128)} %constant.12.clone.share_ref, bf16[256,512]{1,0:T(8,128)(2,1)} %constant.13.clone.inner_ref, ...), custom_call_target="tpu_custom_call" | custom-call | tf_op jit(solution)/shard_map/pallas_call | solution.py:414
  23.0 1.4 %copy.9 = f32[1,4,4,4,128]{4,3,2,1,0:T(4,128)} copy(f32[1,4,4,4,128]{4,3,2,1,0:T(4,128)} %bitcast.1) | data formatting | bytes 65536

commit v2 on v1

--- a/solution.py
+++ b/solution.py
@@ -27,6 +27,7 @@
 BLOCK = ROWS * TILE
 PAIR = CH * CH
 N_TM = 4
+ROW = 8
 
 
 def tables(segments):
@@ -117,7 +118,7 @@
         rows[pl.ds(RADIX + m, ROWS, stride=TILE), :] = im[m] * scale
 
 
-def pair_cross(white, left, right, cross):
+def pair_cross(white, left, right, cross, place):
     def body(s, total):
         def halves(slot, channel):
             start = pl.multiple_of(slot * BLOCK + (channel * SEG + s) * TILE, TILE)
@@ -136,41 +137,51 @@
         return tuple(out)
 
     zero = jnp.zeros((RADIX, LANES), jnp.float32)
-    total = lax.fori_loop(0, SEG, body, (zero,) * (2 * PAIR))
+    total = lax.fori_loop(0, SEG, body, (zero,) * (2 * PAIR), unroll=True)
     for p in range(PAIR):
-        cross[p * RADIX : (p + 1) * RADIX, :] = total[2 * p]
-        cross[(PAIR + p) * RADIX : (PAIR + p + 1) * RADIX, :] = total[2 * p + 1]
-
-
-def pair_lags(white, left, right, cross, inner, outer):
-    pair_cross(white, left, right, cross)
-    re = [cross[pl.ds(m, PAIR, stride=RADIX), :] for m in range(RADIX)]
-    im = [cross[pl.ds(PAIR * RADIX + m, PAIR, stride=RADIX), :] for m in range(RADIX)]
-    parts = [jnp.concatenate(re, axis=0), jnp.concatenate(im, axis=0)]
+        for part in (0, 1):
+            start = ((2 * place + part) * PAIR + p) * RADIX
+            cross[start : start + RADIX, :] = total[2 * p + part]
+
+
+def pair_lags(white, pairs, cross, inner, outer):
+    for place, (left, right) in enumerate(pairs):
+        pair_cross(white, left, right, cross, place)
+    parts = []
+    for part in (0, 1):
+        rows = [
+            cross[pl.ds((2 * place + part) * PAIR * RADIX + m, PAIR, stride=RADIX), :]
+            for m in range(RADIX)
+            for place in range(len(pairs))
+        ]
+        parts.append(jnp.concatenate(rows, axis=0))
     spread = jnp.dot(
         jnp.concatenate(parts, axis=1).astype(jnp.bfloat16),
         inner[...],
         preferred_element_type=jnp.float32,
     )
+    rows = len(pairs) * PAIR
     out = []
     for row in range(N_TM):
         total = None
         for m in range(RADIX):
             lanes = slice(row * LANES, (row + 1) * LANES)
             at = row % 2 * LANES
-            re = spread[m * PAIR : (m + 1) * PAIR, at : at + LANES]
-            im = spread[m * PAIR : (m + 1) * PAIR, POINTS + at : POINTS + at + LANES]
+            re = spread[m * rows : (m + 1) * rows, at : at + LANES]
+            im = spread[m * rows : (m + 1) * rows, POINTS + at : POINTS + at + LANES]
             term = re * outer[m : m + 1, lanes] - im * outer[RADIX + m : RADIX + m + 1, lanes]
             total = term if total is None else total + term
         out.append(total)
-    return out
+    return [
+        [total[place * PAIR : (place + 1) * PAIR, :] for total in out] for place in range(len(pairs))
+    ]
 
 
 def kernel(
     chips, samples_ref, owner_ref, twiddle_ref, dft_ref, share_ref, inner_ref, outer_ref, out_ref,
     samples, twiddle, dft, share, inner, outer, owner, z, y, rows, white, cross, result,
     from_a, from_x, from_b, from_y,
-    load_sem, send_sem, recv_sem, sum_send, sum_recv, ready,
+    load_sem, send_sem, recv_sem, sum_send, sum_recv, ready, ready_two,
 ):
     position, t = lax.axis_index("chan"), lax.axis_index("tm")
     q, e = position // 2, lax.rem(position, 2)
@@ -187,15 +198,21 @@
     def greet(target):
         pl.semaphore_signal(barrier, inc=1, device_id=target, device_id_type=MESH)
 
-    has_before, has_after = q > 0, q < chips - 1
+    last = q // (chips - 1)
+    column = lax.rem(q, ROW)
+    has_before, has_after = q > 0, last == 0
+    opens, closes = column == 0, column == ROW - 1
+    joins = jnp.logical_and(closes, has_after)
+    lends = jnp.logical_and(column == 1, q > ROW)
+    two_before, two_after = lax.rem(q + chips - 2, chips), lax.rem(q + 2, chips)
 
     @pl.when(has_before)
     def _():
-        greet(device(before, 1, t))
-
-    @pl.when(jnp.logical_and(has_before, e == 0))
-    def _():
-        greet(device(before, 0, t))
+        greet(device(before, e, t))
+
+    @pl.when(lends)
+    def _():
+        greet(device(two_before, e, t))
 
     greet(device(q, 1 - e, t))
     for step in range(1, N_TM):
@@ -211,12 +228,18 @@
     ]
     for load in loads:
         load.start()
-    last = q // (chips - 1)
-    pl.semaphore_wait(barrier, 1 + 2 * (N_TM - 1) + (1 - last) * (1 + e))
+    pl.semaphore_wait(barrier, 1 + 2 * (N_TM - 1) + (1 - last) * (1 + column // (ROW - 1)))
+
+    def tell(semaphore, target):
+        pl.semaphore_signal(semaphore, inc=1, device_id=target, device_id_type=MESH)
 
     @pl.when(has_after)
     def _():
-        pl.semaphore_signal(ready, inc=1, device_id=device(after, e, t), device_id_type=MESH)
+        tell(ready, device(after, e, t))
+
+    @pl.when(joins)
+    def _():
+        tell(ready_two, device(two_after, e, t))
 
     for load in loads[:4]:
         load.wait()
@@ -233,9 +256,14 @@
         )
 
     to_after = send(2 + e, 1, device(after, e, t))
-    to_after_other = send(3, 3, device(after, 0, t))
     to_other = send(e, 2, device(q, 1 - e, t))
     to_before = send(4, 0, device(before, e, t))
+    to_two_before = send(5, 4, device(two_before, e, t))
+    passed = pl.ds(3 * BLOCK, BLOCK)
+    pass_on = pltpu.make_async_remote_copy(
+        src_ref=white.at[passed, :], dst_ref=white.at[passed, :], send_sem=send_sem.at[3],
+        recv_sem=recv_sem.at[3], device_id=device(q, 1 - e, t), device_id_type=MESH,
+    )
 
     def put(place, value):
         for row in range(N_TM):
@@ -244,22 +272,23 @@
     def chosen(by, yes, no):
         return [jnp.where(by, a, b) for a, b in zip(yes, no)]
 
-    def lagged(left, right):
-        return pair_lags(white, left, right, cross, inner, outer)
+    def lagged(*pairs):
+        return pair_lags(white, pairs, cross, inner, outer)
 
     def hand(core, step, n):
         row = other(step)
+        near, far = n < 2, n < 4
         if core == 0:
-            place, size, buffer, kind = n, 1, (from_a, from_b)[n // 2], n // 2 * 2
+            place, size, buffer, kind = n, 1, (from_a if near else from_b), (0 if near else 2)
         else:
-            place, size = (0, 1, 3, 3)[n], 2 - n // 2
-            buffer, kind = (from_x, from_y)[n // 2], 1 + n // 2 * 2
+            place, size = (0, 1, 3, 3, 4, 4)[n], 2 if near else 1
+            buffer, kind = (from_x if near else from_y), (1 if near else 3)
         return pltpu.make_async_remote_copy(
             src_ref=result.at[row, pl.ds(place * PAIR, size * PAIR), :],
             dst_ref=buffer.at[t],
             send_sem=sum_send.at[step, n],
             recv_sem=sum_recv.at[kind, t],
-            device_id=device(q if n < 2 else before, n % 2, row),
+            device_id=device(before if far and not near else q, n % 2, row),
             device_id_type=MESH,
         )
 
@@ -268,7 +297,7 @@
             hand(core, step, n)
             for step in (2, 1, 3, 0)
             for n in targets
-            if step > 0 or n != core
+            if step > 0 or n % 2 != core or 2 <= n < 4
         ]
 
     def start(copies):
@@ -282,71 +311,121 @@
     swap = owner[2 * q] != 2 * q
     swap_before = owner[2 * before] != 2 * before
 
-    to_other.start()
-
-    @pl.when(has_after)
-    def _():
-        @pl.when(e == 1)
-        def _():
-            to_after_other.start()
-
-        to_after.start()
-
-    @pl.when(has_before)
-    def _():
-        pl.semaphore_wait(ready, 1)
-        to_before.start()
-
-    to_other.wait_recv()
-
-    @pl.when(e == 0)
-    def _():
+    def first_core():
+        @pl.when(has_before)
+        def _():
+            @pl.when(opens)
+            def _():
+                to_after.start()
+
+            pl.semaphore_wait(ready, 1)
+            to_before.start()
+
+        to_other.start()
+
+        @pl.when(jnp.logical_not(jnp.logical_or(closes, jnp.logical_and(opens, has_before))))
+        def _():
+            to_after.start()
+
+        to_other.wait_recv()
+
         @pl.when(has_after)
         def _():
             to_before.wait_recv()
 
-        one, two = lagged(0, 4), lagged(1, 4)
+        one, two = lagged((0, 4), (1, 4))
         put(0, chosen(swap, two, one))
         put(1, chosen(swap, one, two))
         near = start(hands(0, (0, 1)))
         from_a[t] = result[t, :PAIR, :]
 
-        @pl.when(has_before)
+        @pl.when(jnp.logical_not(opens))
         def _():
             to_after.wait_recv()
-            to_after_other.wait_recv()
-            one, two = lagged(2, 4), lagged(3, 4)
+            pass_on.wait_recv()
+            one, two = lagged((2, 4), (3, 4))
             put(2, chosen(swap_before, two, one))
             put(3, chosen(swap_before, one, two))
-            for copy in start(hands(0, (2, 3))):
-                copy.wait_send()
-
-        for copy in near:
-            copy.wait_send()
-
-    @pl.when(e == 1)
-    def _():
-        put(1, lagged(0, 1))
+            start(hands(0, (2, 3)))
+
+        @pl.when(joins)
+        def _():
+            to_two_before.wait_recv()
+            one, two = lagged((0, 5), (1, 5))
+            put(4, chosen(swap, two, one))
+            put(5, chosen(swap, one, two))
+            start(hands(0, (4, 5)))
+            from_b[t] = result[t, 4 * PAIR : 5 * PAIR, :]
+
+        return near
+
+    def second_core():
+        @pl.when(jnp.logical_not(closes))
+        def _():
+            to_after.start()
+
+        to_other.start()
+
+        @pl.when(has_before)
+        def _():
+            pl.semaphore_wait(ready, 1)
+            to_before.start()
+
+        to_other.wait_recv()
+        put(1, lagged((0, 1))[0])
+
+        @pl.when(jnp.logical_not(opens))
+        def _():
+            to_after.wait_recv()
+            pass_on.start()
 
         @pl.when(has_after)
         def _():
             to_before.wait_recv()
 
-        one, two = lagged(0, 4), lagged(1, 4)
+        @pl.when(jnp.logical_not(opens))
+        def _():
+            put(3, lagged((3, 4))[0])
+            start(hands(1, (2, 3)))
+
+        one, two = lagged((0, 4), (1, 4))
         put(0, chosen(swap, two, one))
         put(2, chosen(swap, one, two))
         near = start(hands(1, (0, 1)))
         from_x[t] = result[t, PAIR : 3 * PAIR, :]
 
-        @pl.when(has_before)
-        def _():
-            to_after.wait_recv()
-            put(3, lagged(3, 4))
-            for copy in start(hands(1, (2, 3))):
+        @pl.when(joins)
+        def _():
+            to_two_before.wait_recv()
+            put(4, lagged((1, 5))[0])
+            start(hands(1, (4, 5)))
+            from_y[t] = result[t, 4 * PAIR : 5 * PAIR, :]
+
+        return near
+
+    for core, run in ((0, first_core), (1, second_core)):
+
+        @pl.when(e == core)
+        def _():
+            near = run()
+
+            @pl.when(lends)
+            def _():
+                pl.semaphore_wait(ready_two, 1)
+                to_two_before.start()
+
+            for copy in near:
                 copy.wait_send()
 
-        for copy in near:
-            copy.wait_send()
+            @pl.when(jnp.logical_not(opens))
+            def _():
+                for copy in hands(core, (2, 3)):
+                    copy.wait_send()
+
+            @pl.when(joins)
+            def _():
+                for copy in hands(core, (4, 5)):
+                    copy.wait_send()
 
     def arrived(size, buffer, n, row):
         return pltpu.make_async_remote_copy(
@@ -363,9 +442,17 @@
 
     @pl.when(has_after)
     def _():
-        for row in range(N_TM):
-            arrived(PAIR, from_b, 2, row).wait_recv()
-            arrived(PAIR, from_y, 3, row).wait_recv()
+        for step in range(1, N_TM):
+            arrived(PAIR, from_b, 2, other(step)).wait_recv()
+            arrived(PAIR, from_y, 3, other(step)).wait_recv()
+
+    @pl.when(jnp.logical_or(jnp.logical_not(closes), jnp.logical_and(joins, e == 1)))
+    def _():
+        arrived(PAIR, from_b, 2, t).wait_recv()
+
+    @pl.when(jnp.logical_or(jnp.logical_not(closes), jnp.logical_and(joins, e == 0)))
+    def _():
+        arrived(PAIR, from_y, 3, t).wait_recv()
 
     @pl.when(e == 1)
     def _():
@@ -398,13 +485,17 @@
     def _():
         to_before.wait_send()
 
-    @pl.when(has_after)
+    @pl.when(lends)
+    def _():
+        to_two_before.wait_send()
+
+    @pl.when(jnp.logical_not(closes))
     def _():
         to_after.wait_send()
 
-        @pl.when(e == 1)
-        def _():
-            to_after_other.wait_send()
+    @pl.when(jnp.logical_and(e == 1, jnp.logical_not(opens)))
+    def _():
+        pass_on.wait_send()
 
 
 def shards(chips, samples, block_owner):
@@ -427,18 +518,19 @@
             pltpu.VMEM((RADIX * ROWS, 2 * POINTS), jnp.float32),
             pltpu.VMEM((RADIX * ROWS, 2 * LANES), jnp.float32),
             pltpu.VMEM((BLOCK, LANES), jnp.float32),
-            pltpu.VMEM((5 * BLOCK, LANES), jnp.bfloat16),
-            pltpu.VMEM((2 * PAIR * RADIX, LANES), jnp.float32),
-            pltpu.VMEM((N_TM, BAND * PAIR, LANES), jnp.float32),
+            pltpu.VMEM((6 * BLOCK, LANES), jnp.bfloat16),
+            pltpu.VMEM((4 * PAIR * RADIX, LANES), jnp.float32),
+            pltpu.VMEM((N_TM, 6 * PAIR, LANES), jnp.float32),
             pltpu.VMEM((N_TM, PAIR, LANES), jnp.float32),
             pltpu.VMEM((N_TM, 2 * PAIR, LANES), jnp.float32),
             pltpu.VMEM((N_TM, PAIR, LANES), jnp.float32),
             pltpu.VMEM((N_TM, PAIR, LANES), jnp.float32),
             pltpu.SemaphoreType.DMA((7,)),
-            pltpu.SemaphoreType.DMA((4,)),
-            pltpu.SemaphoreType.DMA((4,)),
-            pltpu.SemaphoreType.DMA((N_TM, 4)),
+            pltpu.SemaphoreType.DMA((5,)),
+            pltpu.SemaphoreType.DMA((5,)),
+            pltpu.SemaphoreType.DMA((N_TM, 6)),
             pltpu.SemaphoreType.DMA((4, N_TM)),
+            pltpu.SemaphoreType.REGULAR,
             pltpu.SemaphoreType.REGULAR,
         ],
         compiler_params=pltpu.CompilerParams(collective_id=0, has_side_effects=True),

time: 24.5 us -> 23.2 us (0.947)
  the two profiles are of different devices: /device:TPU:48 before, /device:TPU:1 now
where the time goes in v2:
time: 23.2 us; the launch traced here: 23 us
  Pallas kernels  21.6 us (93%)
  local copies, waits for them, and re-layouts  1.38 us (6%)
    pallas_call x1, Pallas kernels, shards(): pl.pallas_call(functools.partial(kernel, chips), out_shape=jax.ShapeDtype...  21.6 us
    unnamed x1, local copies, waits for them, and re-layouts  1.38 us

profile of v2, /device:TPU:1, one launch (start us, length us, event | category | flops | bytes accessed | tf_op | source)
XLA Modules:
  0.0 23.0 jit_solution(9684617332749842585)
XLA Ops:
  0.0 21.6 %shard_map.73 = f32[64,128]{1,0:T(8,128)} custom-call(f32[4,8,2048]{2,1,0:T(8,128)} %samples_ref.1, s32[128]{0:T(128)} %owner_ref.1, f32[16,256]{1,0:T(8,128)} %constant.10.clone.twiddle_ref, f32[512,256]{1,0:T(8,128)} %constant.11.clone.dft_ref, f32[8,128]{1,0:T(8,128)} %constant.12.clone.share_ref, bf16[256,512]{1,0:T(8,128)(2,1)} %constant.13.clone.inner_ref, ...), custom_call_target="tpu_custom_call" | custom-call | tf_op jit(solution)/shard_map/pallas_call | solution.py:505
  21.6 1.4 %copy.9 = f32[1,4,4,4,128]{4,3,2,1,0:T(4,128)} copy(f32[1,4,4,4,128]{4,3,2,1,0:T(4,128)} %bitcast.1) | data formatting | bytes 65536

commit v3 on v2

--- a/solution.py
+++ b/solution.py
@@ -25,6 +25,7 @@
 RADIX = 8
 POINTS = NSEG // RADIX
 BLOCK = ROWS * TILE
+HALF = BLOCK // 2
 PAIR = CH * CH
 N_TM = 4
 ROW = 8
@@ -88,24 +89,29 @@
     return out
 
 
-def whiten(samples, twiddle, dft, share, z, y, rows):
-    x = [samples[:, :, t * POINTS : (t + 1) * POINTS].reshape(ROWS, POINTS) for t in range(RADIX)]
+def whiten(samples, twiddle, dft, share, z, y, rows, first, channels):
+    size = channels * SEG
+    x = [
+        samples[first : first + channels, :, t * POINTS : (t + 1) * POINTS].reshape(size, POINTS)
+        for t in range(RADIX)
+    ]
     total = ((x[0] + x[1]) + (x[2] + x[3])) + ((x[4] + x[5]) + (x[6] + x[7]))
     mean = jnp.sum(total, axis=1, keepdims=True) * (1.0 / NSEG)
     x = [part - mean for part in x]
     for k1, (re, im) in enumerate(radix_stage(x, twiddle)):
-        z[k1 * ROWS : (k1 + 1) * ROWS, :POINTS] = re
-        z[k1 * ROWS : (k1 + 1) * ROWS, POINTS:] = im
-    y[...] = jnp.dot(
-        z[...], dft[...], precision=lax.Precision.HIGHEST, preferred_element_type=jnp.float32
+        z[k1 * size : (k1 + 1) * size, :POINTS] = re
+        z[k1 * size : (k1 + 1) * size, POINTS:] = im
+    spectra = slice(0, RADIX * size)
+    y[spectra, :] = jnp.dot(
+        z[spectra, :], dft[...], precision=lax.Precision.HIGHEST, preferred_element_type=jnp.float32
     )
-    re = [y[m * ROWS : (m + 1) * ROWS, :LANES] for m in range(RADIX)]
-    im = [y[m * ROWS : (m + 1) * ROWS, LANES:] for m in range(RADIX)]
-    size = [jnp.sqrt(r * r + i * i) for r, i in zip(re, im)]
-    before, after = [size[0]], [size[-1]]
+    re = [y[m * size : (m + 1) * size, :LANES] for m in range(RADIX)]
+    im = [y[m * size : (m + 1) * size, LANES:] for m in range(RADIX)]
+    length = [jnp.sqrt(r * r + i * i) for r, i in zip(re, im)]
+    before, after = [length[0]], [length[-1]]
     for m in range(1, RADIX):
-        before.append(before[-1] + size[m])
-        after.append(after[-1] + size[RADIX - 1 - m])
+        before.append(before[-1] + length[m])
+        after.append(after[-1] + length[RADIX - 1 - m])
     after = after[::-1]
     whole = before[-1]
     middle = whole
@@ -114,8 +120,9 @@
     for m in range(RADIX):
         window = middle + (shifted(before[m], -4) + shifted(after[m], 4))
         scale = 1.0 / (window * share[m : m + 1, :] + EPSILON)
-        rows[pl.ds(m, ROWS, stride=TILE), :] = re[m] * scale
-        rows[pl.ds(RADIX + m, ROWS, stride=TILE), :] = im[m] * scale
+        start = first * SEG * TILE + m
+        rows[pl.ds(start, size, stride=TILE), :] = re[m] * scale
+        rows[pl.ds(start + RADIX, size, stride=TILE), :] = im[m] * scale
 
 
 def pair_cross(white, left, right, cross, place):
@@ -193,32 +200,6 @@
     def other(step):
         return lax.rem(t + step, N_TM)
 
-    barrier = pltpu.get_barrier_semaphore()
-
-    def greet(target):
-        pl.semaphore_signal(barrier, inc=1, device_id=target, device_id_type=MESH)
-
-    last = q // (chips - 1)
-    column = lax.rem(q, ROW)
-    has_before, has_after = q > 0, last == 0
-    opens, closes = column == 0, column == ROW - 1
-    joins = jnp.logical_and(closes, has_after)
-    lends = jnp.logical_and(column == 1, q > ROW)
-    two_before, two_after = lax.rem(q + chips - 2, chips), lax.rem(q + 2, chips)
-
-    @pl.when(has_before)
-    def _():
-        greet(device(before, e, t))
-
-    @pl.when(lends)
-    def _():
-        greet(device(two_before, e, t))
-
-    greet(device(q, 1 - e, t))
-    for step in range(1, N_TM):
-        for core in (0, 1):
-            greet(device(q, core, other(step)))
-
     loads = [
         pltpu.make_async_copy(src, dst, load_sem.at[n])
         for n, (src, dst) in enumerate(
@@ -228,6 +209,33 @@
     ]
     for load in loads:
         load.start()
+
+    barrier = pltpu.get_barrier_semaphore()
+
+    def greet(target):
+        pl.semaphore_signal(barrier, inc=1, device_id=target, device_id_type=MESH)
+
+    last = q // (chips - 1)
+    column = lax.rem(q, ROW)
+    has_before, has_after = q > 0, last == 0
+    opens, closes = column == 0, column == ROW - 1
+    joins = jnp.logical_and(closes, has_after)
+    lends = jnp.logical_and(column == 1, q > ROW)
+    two_before, two_after = lax.rem(q + chips - 2, chips), lax.rem(q + 2, chips)
+
+    @pl.when(has_before)
+    def _():
+        greet(device(before, e, t))
+
+    @pl.when(lends)
+    def _():
+        greet(device(two_before, e, t))
+
+    greet(device(q, 1 - e, t))
+    for step in range(1, N_TM):
+        for core in (0, 1):
+            greet(device(q, core, other(step)))
+
     pl.semaphore_wait(barrier, 1 + 2 * (N_TM - 1) + (1 - last) * (1 + column // (ROW - 1)))
 
     def tell(semaphore, target):
@@ -244,30 +252,78 @@
     for load in loads[:4]:
         load.wait()
 
-    whiten(samples, twiddle, dft, share, z, y, rows)
-    own = pl.ds(pl.multiple_of(e * BLOCK, BLOCK), BLOCK)
-    white[own, :] = rows[...].astype(jnp.bfloat16)
-
-    def send(slot, n, target):
-        place = pl.ds(pl.multiple_of(slot * BLOCK, BLOCK), BLOCK)
-        return pltpu.make_async_remote_copy(
-            src_ref=white.at[own, :], dst_ref=white.at[place, :], send_sem=send_sem.at[n],
-            recv_sem=recv_sem.at[n], device_id=target, device_id_type=MESH,
-        )
-
-    to_after = send(2 + e, 1, device(after, e, t))
-    to_other = send(e, 2, device(q, 1 - e, t))
-    to_before = send(4, 0, device(before, e, t))
-    to_two_before = send(5, 4, device(two_before, e, t))
-    passed = pl.ds(3 * BLOCK, BLOCK)
-    pass_on = pltpu.make_async_remote_copy(
-        src_ref=white.at[passed, :], dst_ref=white.at[passed, :], send_sem=send_sem.at[3],
-        recv_sem=recv_sem.at[3], device_id=device(q, 1 - e, t), device_id_type=MESH,
-    )
+    class Halves:
+        def __init__(self, source, slot, n, target):
+            self.copies = []
+            for half in (0, 1):
+                start = pl.multiple_of(source * BLOCK + half * HALF, HALF)
+                place = pl.multiple_of(slot * BLOCK + half * HALF, HALF)
+                self.copies.append(
+                    pltpu.make_async_remote_copy(
+                        src_ref=white.at[pl.ds(start, HALF), :],
+                        dst_ref=white.at[pl.ds(place, HALF), :],
+                        send_sem=send_sem.at[n, half],
+                        recv_sem=recv_sem.at[n, half],
+                        device_id=target,
+                        device_id_type=MESH,
+                    )
+                )
+
+        def start(self):
+            for copy in self.copies:
+                copy.start()
+
+        def wait_recv(self):
+            for copy in self.copies:
+                copy.wait_recv()
+
+        def wait_send(self):
+            for copy in self.copies:
+                copy.wait_send()
+
+    to_after = Halves(e, 2 + e, 1, device(after, e, t))
+    to_other = Halves(e, e, 2, device(q, 1 - e, t))
+    to_before = Halves(e, 4, 0, device(before, e, t))
+    to_two_before = Halves(e, 5, 4, device(two_before, e, t))
+    pass_on = Halves(3, 3, 3, device(q, 1 - e, t))
+
+    def ahead(half):
+        @pl.when(jnp.logical_not(closes))
+        def _():
+            to_after.copies[half].start()
+
+    def back(half):
+        @pl.when(jnp.logical_not(opens))
+        def _():
+            if half == 0:
+                pl.semaphore_wait(ready, 1)
+            to_before.copies[half].start()
+
+    for half in (0, 1):
+        whiten(samples, twiddle, dft, share, z, y, rows, half * CH // 2, CH // 2)
+        start = pl.multiple_of(e * BLOCK + half * HALF, HALF)
+        white[pl.ds(start, HALF), :] = rows[half * HALF : (half + 1) * HALF, :].astype(jnp.bfloat16)
+
+        @pl.when(e == 0)
+        def _():
+            back(half)
+            ahead(half)
+
+        @pl.when(e == 1)
+        def _():
+            ahead(half)
+            back(half)
+
+        to_other.copies[half].start()
+
+    @pl.when(jnp.logical_and(opens, has_before))
+    def _():
+        pl.semaphore_wait(ready, 1)
+        to_before.start()
 
     def put(place, value):
         for row in range(N_TM):
-            result[row, place * PAIR : (place + 1) * PAIR, :] = value[row]
+            result[row, place * PAIR : (place + 1) * PAIR, :] = value[row].astype(jnp.bfloat16)
 
     def chosen(by, yes, no):
         return [jnp.where(by, a, b) for a, b in zip(yes, no)]
@@ -312,32 +368,11 @@
     swap_before = owner[2 * before] != 2 * before
 
     def first_core():
-        @pl.when(has_before)
-        def _():
-            @pl.when(opens)
-            def _():
-                to_after.start()
-
-            pl.semaphore_wait(ready, 1)
-            to_before.start()
-
-        to_other.start()
-
-        @pl.when(jnp.logical_not(jnp.logical_or(closes, jnp.logical_and(opens, has_before))))
-        def _():
-            to_after.start()
-
         to_other.wait_recv()
 
         @pl.when(has_after)
         def _():
             to_before.wait_recv()
-
-        one, two = lagged((0, 4), (1, 4))
-        put(0, chosen(swap, two, one))
-        put(1, chosen(swap, one, two))
-        near = start(hands(0, (0, 1)))
-        from_a[t] = result[t, :PAIR, :]
 
         @pl.when(jnp.logical_not(opens))
         def _():
@@ -348,6 +383,12 @@
             put(3, chosen(swap_before, one, two))
             start(hands(0, (2, 3)))
 
+        one, two = lagged((0, 4), (1, 4))
+        put(0, chosen(swap, two, one))
+        put(1, chosen(swap, one, two))
+        near = start(hands(0, (0, 1)))
+        from_a[t] = result[t, :PAIR, :]
+
         @pl.when(joins)
         def _():
             to_two_before.wait_recv()
@@ -360,24 +401,14 @@
         return near
 
     def second_core():
-        @pl.when(jnp.logical_not(closes))
-        def _():
-            to_after.start()
-
-        to_other.start()
-
-        @pl.when(has_before)
-        def _():
-            pl.semaphore_wait(ready, 1)
-            to_before.start()
-
         to_other.wait_recv()
         put(1, lagged((0, 1))[0])
 
         @pl.when(jnp.logical_not(opens))
         def _():
-            to_after.wait_recv()
-            pass_on.start()
+            for copy, passed in zip(to_after.copies, pass_on.copies):
+                copy.wait_recv()
+                passed.start()
 
         @pl.when(has_after)
         def _():
@@ -463,7 +494,8 @@
         arrived(2 * PAIR, from_x, 1, t).wait_recv()
 
     def summed(buffer):
-        return (buffer[0] + buffer[1]) + (buffer[2] + buffer[3])
+        first, second, third, fourth = [buffer[row].astype(jnp.float32) for row in range(N_TM)]
+        return (first + second) + (third + fourth)
 
     a, x, b, last = summed(from_a), summed(from_x), summed(from_b), summed(from_y)
     flip = e == 1
@@ -504,7 +536,7 @@
     stay = pl.BlockSpec(memory_space=pltpu.HBM)
     out = pl.pallas_call(
         functools.partial(kernel, chips),
-        out_shape=jax.ShapeDtypeStruct((BAND * PAIR, LANES), jnp.float32),
+        out_shape=pltpu.VMEM((BAND * PAIR, LANES), jnp.float32),
         in_specs=[stay] * 7,
         out_specs=pl.BlockSpec(memory_space=pltpu.VMEM),
         scratch_shapes=[
@@ -520,20 +552,22 @@
             pltpu.VMEM((BLOCK, LANES), jnp.float32),
             pltpu.VMEM((6 * BLOCK, LANES), jnp.bfloat16),
             pltpu.VMEM((4 * PAIR * RADIX, LANES), jnp.float32),
-            pltpu.VMEM((N_TM, 6 * PAIR, LANES), jnp.float32),
-            pltpu.VMEM((N_TM, PAIR, LANES), jnp.float32),
-            pltpu.VMEM((N_TM, 2 * PAIR, LANES), jnp.float32),
-            pltpu.VMEM((N_TM, PAIR, LANES), jnp.float32),
-            pltpu.VMEM((N_TM, PAIR, LANES), jnp.float32),
+            pltpu.VMEM((N_TM, 6 * PAIR, LANES), jnp.bfloat16),
+            pltpu.VMEM((N_TM, PAIR, LANES), jnp.bfloat16),
+            pltpu.VMEM((N_TM, 2 * PAIR, LANES), jnp.bfloat16),
+            pltpu.VMEM((N_TM, PAIR, LANES), jnp.bfloat16),
+            pltpu.VMEM((N_TM, PAIR, LANES), jnp.bfloat16),
             pltpu.SemaphoreType.DMA((7,)),
-            pltpu.SemaphoreType.DMA((5,)),
-            pltpu.SemaphoreType.DMA((5,)),
+            pltpu.SemaphoreType.DMA((5, 2)),
+            pltpu.SemaphoreType.DMA((5, 2)),
             pltpu.SemaphoreType.DMA((N_TM, 6)),
             pltpu.SemaphoreType.DMA((4, N_TM)),
             pltpu.SemaphoreType.REGULAR,
             pltpu.SemaphoreType.REGULAR,
         ],
-        compiler_params=pltpu.CompilerParams(collective_id=0, has_side_effects=True),
+        compiler_params=pltpu.CompilerParams(
+            collective_id=0, has_side_effects=True, vmem_limit_bytes=58 * 1024 * 1024
+        ),
     )(
         samples, block_owner, jnp.asarray(twiddle), jnp.asarray(dft), jnp.asarray(share),
         jnp.asarray(inner), jnp.asarray(outer),

time: 23.2 us -> 20.9 us (0.901)
  Pallas kernels: 21.6 us -> 20.1 us
  local copies, waits for them, and re-layouts: 1.38 us -> 0.62 us
    pallas_call x1, Pallas kernels: 21.6 us -> 20.1 us  [shards(): pl.pallas_call(functools.partial(kernel, chips), out_shape=pltpu.VMEM((BA...]
    unnamed x1, local copies, waits for them, and re-layouts: 1.38 us -> 0.62 us
where the time goes in v3:
time: 20.9 us; the launch traced here: 20.7 us
  Pallas kernels  20.1 us (96%)
  local copies, waits for them, and re-layouts  0.62 us (3%)
    pallas_call x1, Pallas kernels, shards(): pl.pallas_call(functools.partial(kernel, chips), out_shape=pltpu.VMEM((BA...  20.1 us
    unnamed x1, local copies, waits for them, and re-layouts  0.62 us

profile of v3, /device:TPU:1, one launch (start us, length us, event | category | flops | bytes accessed | tf_op | source)
XLA Modules:
  0.0 20.7 jit_solution(16173467186740019873)
XLA Ops:
  0.0 20.1 %shard_map.73 = f32[64,128]{1,0:T(8,128)S(1)} custom-call(f32[4,8,2048]{2,1,0:T(8,128)} %samples_ref.1, s32[128]{0:T(128)} %owner_ref.1, f32[16,256]{1,0:T(8,128)} %constant.10.clone.twiddle_ref, f32[512,256]{1,0:T(8,128)} %constant.11.clone.dft_ref, f32[8,128]{1,0:T(8,128)} %constant.12.clone.share_ref, bf16[256,512]{1,0:T(8,128)(2,1)} %constant.13.clone.inner_ref, ...), custom_call_target="tpu_custom_call" | custom-call | tf_op jit(solution)/shard_map/pallas_call | solution.py:537
  20.1 0.6 %copy.9 = f32[1,4,4,4,128]{4,3,2,1,0:T(4,128)} copy(f32[1,4,4,4,128]{4,3,2,1,0:T(4,128)S(1)} %bitcast.1) | data formatting | bytes 65536

commit v4 on v3

--- a/solution.py
+++ b/solution.py
@@ -188,7 +188,7 @@
     chips, samples_ref, owner_ref, twiddle_ref, dft_ref, share_ref, inner_ref, outer_ref, out_ref,
     samples, twiddle, dft, share, inner, outer, owner, z, y, rows, white, cross, result,
     from_a, from_x, from_b, from_y,
-    load_sem, send_sem, recv_sem, sum_send, sum_recv, ready, ready_two,
+    load_sem, send_sem, recv_sem, sum_send, sum_recv, ready, ready_back, ready_two,
 ):
     position, t = lax.axis_index("chan"), lax.axis_index("tm")
     q, e = position // 2, lax.rem(position, 2)
@@ -219,11 +219,16 @@
     column = lax.rem(q, ROW)
     has_before, has_after = q > 0, last == 0
     opens, closes = column == 0, column == ROW - 1
+    first = q == 0
     joins = jnp.logical_and(closes, has_after)
     lends = jnp.logical_and(column == 1, q > ROW)
     two_before, two_after = lax.rem(q + chips - 2, chips), lax.rem(q + 2, chips)
 
-    @pl.when(has_before)
+    @pl.when(jnp.logical_not(closes))
+    def _():
+        greet(device(after, e, t))
+
+    @pl.when(jnp.logical_and(opens, has_before))
     def _():
         greet(device(before, e, t))
 
@@ -236,17 +241,19 @@
         for core in (0, 1):
             greet(device(q, core, other(step)))
 
-    pl.semaphore_wait(barrier, 1 + 2 * (N_TM - 1) + (1 - last) * (1 + column // (ROW - 1)))
+    in_row, at_end = (column + ROW - 1) // ROW, column // (ROW - 1)
+    pl.semaphore_wait(barrier, 1 + 2 * (N_TM - 1) + in_row + 2 * (1 - last) * at_end)
 
     def tell(semaphore, target):
         pl.semaphore_signal(semaphore, inc=1, device_id=target, device_id_type=MESH)
 
-    @pl.when(has_after)
-    def _():
-        tell(ready, device(after, e, t))
+    @pl.when(jnp.logical_not(opens))
+    def _():
+        tell(ready, device(before, e, t))
 
     @pl.when(joins)
     def _():
+        tell(ready_back, device(after, e, t))
         tell(ready_two, device(two_after, e, t))
 
     for load in loads[:4]:
@@ -287,38 +294,31 @@
     to_two_before = Halves(e, 5, 4, device(two_before, e, t))
     pass_on = Halves(3, 3, 3, device(q, 1 - e, t))
 
-    def ahead(half):
-        @pl.when(jnp.logical_not(closes))
-        def _():
-            to_after.copies[half].start()
-
-    def back(half):
-        @pl.when(jnp.logical_not(opens))
-        def _():
-            if half == 0:
-                pl.semaphore_wait(ready, 1)
-            to_before.copies[half].start()
-
     for half in (0, 1):
         whiten(samples, twiddle, dft, share, z, y, rows, half * CH // 2, CH // 2)
         start = pl.multiple_of(e * BLOCK + half * HALF, HALF)
         white[pl.ds(start, HALF), :] = rows[half * HALF : (half + 1) * HALF, :].astype(jnp.bfloat16)
 
-        @pl.when(e == 0)
-        def _():
-            back(half)
-            ahead(half)
-
-        @pl.when(e == 1)
-        def _():
-            ahead(half)
-            back(half)
-
-        to_other.copies[half].start()
+        @pl.when(jnp.logical_not(opens))
+        def _():
+            to_before.copies[half].start()
+
+        @pl.when(first)
+        def _():
+            if half == 0:
+                pl.semaphore_wait(ready, 1)
+            to_after.copies[half].start()
+
+    @pl.when(jnp.logical_not(jnp.logical_or(first, closes)))
+    def _():
+        pl.semaphore_wait(ready, 1)
+        to_after.start()
+
+    to_other.start()
 
     @pl.when(jnp.logical_and(opens, has_before))
     def _():
-        pl.semaphore_wait(ready, 1)
+        pl.semaphore_wait(ready_back, 1)
         to_before.start()
 
     def put(place, value):
@@ -343,23 +343,30 @@
             src_ref=result.at[row, pl.ds(place * PAIR, size * PAIR), :],
             dst_ref=buffer.at[t],
             send_sem=sum_send.at[step, n],
-            recv_sem=sum_recv.at[kind, t],
+            recv_sem=sum_recv.at[kind],
             device_id=device(before if far and not near else q, n % 2, row),
             device_id_type=MESH,
         )
 
-    def hands(core, targets):
-        return [
-            hand(core, step, n)
-            for step in (2, 1, 3, 0)
-            for n in targets
-            if step > 0 or n % 2 != core or 2 <= n < 4
-        ]
-
-    def start(copies):
-        for copy in copies:
-            copy.start()
-        return copies
+    def each_hand(core, targets, act):
+        @pl.loop(0, N_TM - 1)
+        def _(turn):
+            for n in targets:
+                act(hand(core, 1 + lax.rem(turn + 1, N_TM - 1), n))
+
+        for n in targets:
+            if n % 2 != core or 2 <= n < 4:
+                act(hand(core, 0, n))
+
+    def start(core, targets):
+        each_hand(core, targets, lambda copy: copy.start())
+
+    def finish(core, targets):
+        each_hand(core, targets, lambda copy: copy.wait_send())
+
+    def keep(buffer, kind, place, size):
+        rows_kept = pl.ds(place * PAIR, size * PAIR)
+        pltpu.make_async_copy(result.at[t, rows_kept, :], buffer.at[t], sum_recv.at[kind]).start()
 
     loads[4].wait()
     loads[5].wait()
@@ -381,13 +388,13 @@
             one, two = lagged((2, 4), (3, 4))
             put(2, chosen(swap_before, two, one))
             put(3, chosen(swap_before, one, two))
-            start(hands(0, (2, 3)))
+            start(0, (2, 3))
 
         one, two = lagged((0, 4), (1, 4))
         put(0, chosen(swap, two, one))
         put(1, chosen(swap, one, two))
-        near = start(hands(0, (0, 1)))
-        from_a[t] = result[t, :PAIR, :]
+        start(0, (0, 1))
+        keep(from_a, 0, 0, 1)
 
         @pl.when(joins)
         def _():
@@ -395,10 +402,8 @@
             one, two = lagged((0, 5), (1, 5))
             put(4, chosen(swap, two, one))
             put(5, chosen(swap, one, two))
-            start(hands(0, (4, 5)))
-            from_b[t] = result[t, 4 * PAIR : 5 * PAIR, :]
-
-        return near
+            start(0, (4, 5))
+            keep(from_b, 2, 4, 1)
 
     def second_core():
         to_other.wait_recv()
@@ -417,81 +422,70 @@
         @pl.when(jnp.logical_not(opens))
         def _():
             put(3, lagged((3, 4))[0])
-            start(hands(1, (2, 3)))
+            start(1, (2, 3))
 
         one, two = lagged((0, 4), (1, 4))
         put(0, chosen(swap, two, one))
         put(2, chosen(swap, one, two))
-        near = start(hands(1, (0, 1)))
-        from_x[t] = result[t, PAIR : 3 * PAIR, :]
+        start(1, (0, 1))
+        keep(from_x, 1, 1, 2)
 
         @pl.when(joins)
         def _():
             to_two_before.wait_recv()
             put(4, lagged((1, 5))[0])
-            start(hands(1, (4, 5)))
-            from_y[t] = result[t, 4 * PAIR : 5 * PAIR, :]
-
-        return near
+            start(1, (4, 5))
+            keep(from_y, 3, 4, 1)
 
     for core, run in ((0, first_core), (1, second_core)):
 
         @pl.when(e == core)
         def _():
-            near = run()
+            run()
 
             @pl.when(lends)
             def _():
                 pl.semaphore_wait(ready_two, 1)
                 to_two_before.start()
 
-            for copy in near:
-                copy.wait_send()
+            finish(core, (0, 1))
 
             @pl.when(jnp.logical_not(opens))
             def _():
-                for copy in hands(core, (2, 3)):
-                    copy.wait_send()
+                finish(core, (2, 3))
 
             @pl.when(joins)
             def _():
-                for copy in hands(core, (4, 5)):
-                    copy.wait_send()
-
-    def arrived(size, buffer, n, row):
-        return pltpu.make_async_remote_copy(
-            src_ref=result.at[0, pl.ds(0, size), :], dst_ref=buffer.at[row],
-            send_sem=sum_send.at[0, n], recv_sem=sum_recv.at[n, row],
-            device_id=device(q, 1 - e, t), device_id_type=MESH,
-        )
-
-    for step in range(N_TM):
-        row = other(step)
-        if step > 0:
-            arrived(PAIR, from_a, 0, row).wait_recv()
-            arrived(2 * PAIR, from_x, 1, row).wait_recv()
+                finish(core, (4, 5))
+
+    to_other.wait_send()
+
+    @pl.when(has_before)
+    def _():
+        to_before.wait_send()
+
+    @pl.when(lends)
+    def _():
+        to_two_before.wait_send()
+
+    @pl.when(jnp.logical_not(closes))
+    def _():
+        to_after.wait_send()
+
+    @pl.when(jnp.logical_and(e == 1, jnp.logical_not(opens)))
+    def _():
+        pass_on.wait_send()
+
+    def arrived(buffer, kind):
+        pltpu.make_async_copy(buffer, buffer, sum_recv.at[kind]).wait()
+
+    arrived(from_a, 0)
+    arrived(from_x, 1)
 
     @pl.when(has_after)
     def _():
-        for step in range(1, N_TM):
-            arrived(PAIR, from_b, 2, other(step)).wait_recv()
-            arrived(PAIR, from_y, 3, other(step)).wait_recv()
-
-    @pl.when(jnp.logical_or(jnp.logical_not(closes), jnp.logical_and(joins, e == 1)))
-    def _():
-        arrived(PAIR, from_b, 2, t).wait_recv()
-
-    @pl.when(jnp.logical_or(jnp.logical_not(closes), jnp.logical_and(joins, e == 0)))
-    def _():
-        arrived(PAIR, from_y, 3, t).wait_recv()
-
-    @pl.when(e == 1)
-    def _():
-        arrived(PAIR, from_a, 0, t).wait_recv()
-
-    @pl.when(e == 0)
-    def _():
-        arrived(2 * PAIR, from_x, 1, t).wait_recv()
+        arrived(from_b, 2)
+        arrived(from_y, 3)
 
     def summed(buffer):
         first, second, third, fourth = [buffer[row].astype(jnp.float32) for row in range(N_TM)]
@@ -510,24 +504,6 @@
         out_ref[n * PAIR : (n + 1) * PAIR, :] = jnp.where(
             block + n + 1 < 2 * chips, value, jnp.zeros_like(value)
         )
-
-    to_other.wait_send()
-
-    @pl.when(has_before)
-    def _():
-        to_before.wait_send()
-
-    @pl.when(lends)
-    def _():
-        to_two_before.wait_send()
-
-    @pl.when(jnp.logical_not(closes))
-    def _():
-        to_after.wait_send()
-
-    @pl.when(jnp.logical_and(e == 1, jnp.logical_not(opens)))
-    def _():
-        pass_on.wait_send()
 
 
 def shards(chips, samples, block_owner):
@@ -561,7 +537,8 @@
             pltpu.SemaphoreType.DMA((5, 2)),
             pltpu.SemaphoreType.DMA((5, 2)),
             pltpu.SemaphoreType.DMA((N_TM, 6)),
-            pltpu.SemaphoreType.DMA((4, N_TM)),
+            pltpu.SemaphoreType.DMA((4,)),
+            pltpu.SemaphoreType.REGULAR,
             pltpu.SemaphoreType.REGULAR,
             pltpu.SemaphoreType.REGULAR,
         ],

time: 20.9 us -> 20.8 us (level)
  no operation moved by 1% of the time
where the time goes in v4:
time: 20.8 us; the launch traced here: 20.7 us
  Pallas kernels  20 us (96%)
  local copies, waits for them, and re-layouts  0.62 us (3%)
    pallas_call x1, Pallas kernels, shards(): pl.pallas_call(functools.partial(kernel, chips), out_shape=pltpu.VMEM((BA...  20 us
    unnamed x1, local copies, waits for them, and re-layouts  0.62 us

profile of v4, /device:TPU:1, one launch (start us, length us, event | category | flops | bytes accessed | tf_op | source)
XLA Modules:
  0.0 20.7 jit_solution(639937154040342403)
XLA Ops:
  0.0 20.0 %shard_map.73 = f32[64,128]{1,0:T(8,128)S(1)} custom-call(f32[4,8,2048]{2,1,0:T(8,128)} %samples_ref.1, s32[128]{0:T(128)} %owner_ref.1, f32[16,256]{1,0:T(8,128)} %constant.10.clone.twiddle_ref, f32[512,256]{1,0:T(8,128)} %constant.11.clone.dft_ref, f32[8,128]{1,0:T(8,128)} %constant.12.clone.share_ref, bf16[256,512]{1,0:T(8,128)(2,1)} %constant.13.clone.inner_ref, ...), custom_call_target="tpu_custom_call" | custom-call | tf_op jit(solution)/shard_map/pallas_call | solution.py:513
  20.0 0.6 %copy.9 = f32[1,4,4,4,128]{4,3,2,1,0:T(4,128)} copy(f32[1,4,4,4,128]{4,3,2,1,0:T(4,128)S(1)} %bitcast.1) | data formatting | bytes 65536

commit v5 on v4

--- a/solution.py
+++ b/solution.py
@@ -224,11 +224,14 @@
     lends = jnp.logical_and(column == 1, q > ROW)
     two_before, two_after = lax.rem(q + chips - 2, chips), lax.rem(q + 2, chips)
 
-    @pl.when(jnp.logical_not(closes))
+    second = q == 1
+    held = jnp.logical_or(second, jnp.logical_and(opens, has_before))
+
+    @pl.when(jnp.logical_not(jnp.logical_or(first, closes)))
     def _():
         greet(device(after, e, t))
 
-    @pl.when(jnp.logical_and(opens, has_before))
+    @pl.when(held)
     def _():
         greet(device(before, e, t))
 
@@ -242,18 +245,25 @@
             greet(device(q, core, other(step)))
 
     in_row, at_end = (column + ROW - 1) // ROW, column // (ROW - 1)
+    is_first = (chips - 1 - q) // (chips - 1)
+    in_row += is_first - ((chips - q) // (chips - 1) - is_first)
     pl.semaphore_wait(barrier, 1 + 2 * (N_TM - 1) + in_row + 2 * (1 - last) * at_end)
 
     def tell(semaphore, target):
         pl.semaphore_signal(semaphore, inc=1, device_id=target, device_id_type=MESH)
 
-    @pl.when(jnp.logical_not(opens))
+    in_line = jnp.logical_not(jnp.logical_or(opens, second))
+
+    @pl.when(in_line)
     def _():
         tell(ready, device(before, e, t))
 
+    @pl.when(jnp.logical_or(first, joins))
+    def _():
+        tell(ready_back, device(after, e, t))
+
     @pl.when(joins)
     def _():
-        tell(ready_back, device(after, e, t))
         tell(ready_two, device(two_after, e, t))
 
     for load in loads[:4]:
@@ -299,14 +309,12 @@
         start = pl.multiple_of(e * BLOCK + half * HALF, HALF)
         white[pl.ds(start, HALF), :] = rows[half * HALF : (half + 1) * HALF, :].astype(jnp.bfloat16)
 
-        @pl.when(jnp.logical_not(opens))
+        @pl.when(in_line)
         def _():
             to_before.copies[half].start()
 
         @pl.when(first)
         def _():
-            if half == 0:
-                pl.semaphore_wait(ready, 1)
             to_after.copies[half].start()
 
     @pl.when(jnp.logical_not(jnp.logical_or(first, closes)))
@@ -316,7 +324,7 @@
 
     to_other.start()
 
-    @pl.when(jnp.logical_and(opens, has_before))
+    @pl.when(held)
     def _():
         pl.semaphore_wait(ready_back, 1)
         to_before.start()

time: 20.8 us -> 20.8 us (level)
  no operation moved by 1% of the time
where the time goes in v5:
time: 20.8 us; the launch traced here: 20.6 us
  Pallas kernels  20 us (96%)
  local copies, waits for them, and re-layouts  0.62 us (3%)
    pallas_call x1, Pallas kernels, shards(): pl.pallas_call(functools.partial(kernel, chips), out_shape=pltpu.VMEM((BA...  20 us
    unnamed x1, local copies, waits for them, and re-layouts  0.62 us

profile of v5, /device:TPU:1, one launch (start us, length us, event | category | flops | bytes accessed | tf_op | source)
XLA Modules:
  0.0 20.6 jit_solution(12525384110129402313)
XLA Ops:
  0.0 20.0 %shard_map.73 = f32[64,128]{1,0:T(8,128)S(1)} custom-call(f32[4,8,2048]{2,1,0:T(8,128)} %samples_ref.1, s32[128]{0:T(128)} %owner_ref.1, f32[16,256]{1,0:T(8,128)} %constant.10.clone.twiddle_ref, f32[512,256]{1,0:T(8,128)} %constant.11.clone.dft_ref, f32[8,128]{1,0:T(8,128)} %constant.12.clone.share_ref, bf16[256,512]{1,0:T(8,128)(2,1)} %constant.13.clone.inner_ref, ...), custom_call_target="tpu_custom_call" | custom-call | tf_op jit(solution)/shard_map/pallas_call | solution.py:521
  20.0 0.6 %copy.9 = f32[1,4,4,4,128]{4,3,2,1,0:T(4,128)} copy(f32[1,4,4,4,128]{4,3,2,1,0:T(4,128)S(1)} %bitcast.1) | data formatting | bytes 65536
